TPU v7x, 128 devices: a whole 4x4x4 slice. The times are simulated.
128 devices in a mesh: sec: 4 (over x_hi, core), dev: 32 (over z, y, x_lo).
Axes of the slice: x: 4 (x_hi: 2, x_lo: 2; x = x_hi * 2 + x_lo), y: 4, z: 4, core: 2. Of those that a mesh axis runs over, the one named last changes fastest.
Arguments:
- queries: bfloat16 [1024, 64, 576], P(('sec', 'dev')), may hold values from -6 to 6
- latent_cache: bfloat16 [1024, 1024, 576], P(('sec', 'dev')), may hold values from -9 to 9
- cache_length: int32 [1024], P(('sec', 'dev')), may hold values from 2 to 1024, as said below
- residual: bfloat16 [1024, 7168], P(('sec', 'dev')), may hold values from -9 to 9
- norm_gain: float32 [7168], replicated, may hold values from 0.1 to 1.9
- value_up: bfloat16 [64, 512, 128], P('dev'), may hold values from -4 to 4
- out_weight: bfloat16 [8192, 7168], P('dev'), may hold values from -0.0625 to 0.0625
- gate_weight: bfloat16 [7168, 8192], P(None, 'dev'), may hold values from -0.0625 to 0.0625
- up_weight: bfloat16 [7168, 8192], P(None, 'dev'), may hold values from -0.0625 to 0.0625
- down_weight: bfloat16 [8192, 7168], P('dev'), may hold values from -0.125 to 0.125
- expert_index: int32 [1024, 2], P(('sec', 'dev')), may hold values from 0 to 3, all different within a row; in each aligned block of 4 rows (0 to 3, 4 to 7, ...) at most 3 rows name the same one
- gate_level: int32 [1024, 2], P(('sec', 'dev')), may hold values from 1 to 4095
Outputs:
- layer_output: bfloat16 [1024, 7168], P(('sec', 'dev'))
Inputs may be any that keep to these rules, and one draw needn't show every extreme that they name: `expert_index`: each token names 2 different experts. The rows of one device form 2 aligned blocks of 4 rows, and within such a block no expert is named more than 3 times. `cache_length`: some request of the first 3 sections holds exactly 1024 live positions.
All inputs are finite; a program needn't handle non-finite values.
Results may differ from a plain program's by a relative error of at most 0.03.
Values may be sent and summed in bfloat16 or wider, within the bound.
A program may use at most 192 MiB of HBM per device.

v0:
```python
import jax
import jax.numpy as jnp
from jax import lax
from jax.sharding import PartitionSpec as P

EXPERTS = 4
TOPK = 2
MICRO = 2
CAP = 3


def from_behind(x, axis, by):
    length = lax.axis_size(axis)
    pairs = [(i, i + by) for i in range(length) if 0 <= i + by < length]
    return lax.ppermute(x, axis, pairs)


def expert_block(expert_rows, gate_weight, up_weight, down_weight):
    gate_hidden = jnp.dot(expert_rows, gate_weight, preferred_element_type=jnp.float32)
    up_hidden = jnp.dot(expert_rows, up_weight, preferred_element_type=jnp.float32)
    activated = (jax.nn.silu(gate_hidden) * up_hidden).astype(jnp.bfloat16)
    return jnp.dot(activated, down_weight, preferred_element_type=jnp.float32).astype(jnp.bfloat16)


def layer_block(
    queries,
    latent_cache,
    cache_length,
    residual,
    norm_gain,
    value_up,
    out_weight,
    gate_weight,
    up_weight,
    down_weight,
    expert_index,
    gate_level,
    groups,
):
    sections = lax.axis_size("sec")
    group_size = lax.axis_size("dev")
    section_index = lax.axis_index("sec")
    attending = section_index < sections - 1
    token_count = queries.shape[0]
    latent_width = value_up.shape[1]
    score_scale = (value_up.shape[2] + queries.shape[2] - latent_width) ** (-0.5)
    width = residual.shape[1]
    scores = (
        jnp.einsum("thc,tpc->thp", queries, latent_cache, preferred_element_type=jnp.float32)
        * score_scale
    )
    position = lax.broadcasted_iota(jnp.int32, (1, 1, latent_cache.shape[1]), 2)
    usable = position < cache_length[:, None, None]
    masked = jnp.where(usable, scores, -1e30)
    highest = jnp.max(masked, axis=2, keepdims=True)
    expos = jnp.where(usable, jnp.exp(masked - highest), 0.0)
    weights = (expos / jnp.sum(expos, axis=2, keepdims=True)).astype(jnp.bfloat16)
    latent_out = jnp.einsum(
        "thp,tpc->thc", weights, latent_cache, preferred_element_type=jnp.float32
    )[:, :, :latent_width].astype(jnp.bfloat16)
    by_heads = lax.all_to_all(latent_out, "dev", split_axis=1, concat_axis=0, tiled=True)
    head_out = jnp.einsum(
        "thc,hcv->thv", by_heads, value_up, preferred_element_type=jnp.float32
    ).astype(jnp.bfloat16)
    head_flat = head_out.reshape(head_out.shape[0], -1)
    attended = lax.psum_scatter(
        jnp.dot(head_flat, out_weight, preferred_element_type=jnp.float32).astype(jnp.bfloat16),
        "dev",
        scatter_dimension=0,
        tiled=True,
    ).astype(jnp.float32)
    stream = (residual.astype(jnp.float32) + attended).astype(jnp.bfloat16)
    stream_float = stream.astype(jnp.float32)
    mean_square = jnp.mean(stream_float * stream_float, axis=1, keepdims=True)
    normed = (stream_float * lax.rsqrt(mean_square + 1e-06) * norm_gain).astype(jnp.bfloat16)
    route_count = token_count * TOPK
    per_micro = token_count // groups
    slot_width = groups * CAP
    flat_expert = expert_index.reshape(route_count)
    route_order = jnp.arange(route_count, dtype=jnp.int32)
    micro_of = route_order // TOPK // per_micro
    earlier = (
        (route_order[:, None] > route_order[None, :])
        & (flat_expert[:, None] == flat_expert[None, :])
        & (micro_of[:, None] == micro_of[None, :])
    )
    rank_in = jnp.sum(earlier.astype(jnp.int32), axis=1)
    target = (flat_expert * slot_width + micro_of * CAP + rank_in).reshape(token_count, TOPK)
    slot_index = jnp.arange(EXPERTS * slot_width, dtype=jnp.int32)
    placing = jnp.any(slot_index[:, None, None] == target[None, :, :], axis=2).astype(jnp.bfloat16)
    levels = gate_level.astype(jnp.float32)
    mix = levels / jnp.sum(levels, axis=1, keepdims=True)
    gathering = jnp.sum(
        jnp.where(slot_index[None, None, :] == target[:, :, None], mix[:, :, None], 0.0), axis=1
    )
    packed = jnp.dot(placing, normed, preferred_element_type=jnp.float32)
    packed = jnp.where(attending, packed, 0.0).astype(jnp.bfloat16)
    slab_count = group_size // EXPERTS
    last_section = sections - 1
    pieces = []
    for source in range(last_section):
        pieces.append(from_behind(packed, "sec", last_section - source))
    stacked = jnp.stack(pieces, axis=0).reshape(last_section, EXPERTS, 1, slot_width, width)
    spread = jnp.broadcast_to(stacked, (last_section, EXPERTS, slab_count, slot_width, width))
    spread = jnp.transpose(spread, (1, 2, 0, 3, 4)).reshape(
        group_size, last_section, slot_width, width
    )
    arrived = lax.all_to_all(spread, "dev", split_axis=0, concat_axis=0, tiled=True)
    partial_out = expert_block(arrived.reshape(-1, width), gate_weight, up_weight, down_weight)
    back = lax.all_to_all(
        partial_out.reshape(group_size, last_section, slot_width, width),
        "dev",
        split_axis=0,
        concat_axis=0,
        tiled=True,
    )
    from_flat = jnp.zeros((group_size, slot_width, width), jnp.bfloat16)
    for source in range(last_section):
        moved = from_behind(back[:, source], "sec", source - last_section)
        from_flat = jnp.where(section_index == source, moved, from_flat)
    from_experts = from_flat.reshape(EXPERTS, slab_count, slot_width, width)
    slab_total = jnp.sum(from_experts.astype(jnp.float32), axis=1).reshape(
        EXPERTS * slot_width, width
    )
    moe = jnp.dot(gathering, slab_total, precision=lax.Precision.HIGHEST)
    result = (stream_float + moe).astype(jnp.bfloat16)
    return jnp.where(attending, result, jnp.zeros_like(result))


def body(
    queries,
    latent_cache,
    cache_length,
    residual,
    norm_gain,
    value_up,
    out_weight,
    gate_weight,
    up_weight,
    down_weight,
    expert_index,
    gate_level,
):
    return layer_block(
        queries,
        latent_cache,
        cache_length,
        residual,
        norm_gain,
        value_up,
        out_weight,
        gate_weight,
        up_weight,
        down_weight,
        expert_index,
        gate_level,
        MICRO,
    )


def solution(mesh):
    placed = (
        P(("sec", "dev"), None, None),
        P(("sec", "dev"), None, None),
        P(("sec", "dev")),
        P(("sec", "dev"), None),
        P(),
        P("dev", None, None),
        P("dev", None),
        P(None, "dev"),
        P(None, "dev"),
        P("dev", None),
        P(("sec", "dev"), None),
        P(("sec", "dev"), None),
    )
    return jax.shard_map(
        body, mesh=mesh, in_specs=placed, out_specs=P(("sec", "dev"), None), check_vma=False
    )
```

profile of v0, /device:TPU:0, one launch (start us, length us, event | category | flops | bytes accessed | tf_op | source)
XLA Modules:
  0.0 691.1 jit_solution(9540365093698168124)
XLA Ops:
  7.6 6.0 fusion.32
  13.6 6.6 fusion.6
  20.6 21.5 %all_to_all.28 = bf16[8,64,512]{2,0,1:T(8,128)(2,1)S(1)} all-to-all(bf16[8,64,512]{2,0,1:T(8,128)(2,1)S(1)} %copy.49), channel_id=1, replica_groups=mesh['sec'=4,'dev'=32] {'dev'}, dimensions={1} | all-to-all | bytes 1048576 | tf_op jit(solution)/shard_map/all_to_all | solution.py:61
  42.5 2.9 convolution_convert_fusion.1
  46.8 168.3 %reduce-scatter.2.cloned.1.call-done = bf16[8,7168]{1,0:T(8,128)(2,1)} async-done(((bf16[256,7168]{1,0:T(8,128)(2,1)}), bf16[8,7168]{1,0:T(8,128)(2,1)}) %reduce-scatter.2.cloned.1.call-update) | async-done | bytes 114704 | tf_op jit(solution)/shard_map/reduce_scatter | solution.py:66
  217.4 1.3 collective-permute-start
  218.7 3.6 collective-permute-start.1
  223.8 6.3 collective-permute-done.1
  230.8 5.4 broadcast_in_dim.67
  236.2 132.8 %all_to_all.29 = bf16[32,3,6,7168]{3,2,1,0:T(8,128)(2,1)} all-to-all(bf16[32,3,6,7168]{3,2,1,0:T(8,128)(2,1)} %bitcast.46), channel_id=1, replica_groups=mesh['sec'=4,'dev'=32] {'dev'}, dimensions={0} | all-to-all | bytes 16515072 | tf_op jit(solution)/shard_map/all_to_all | solution.py:108
  369.0 12.5 %reshape.218 = bf16[576,7168]{1,0:T(8,128)(2,1)} reshape(bf16[32,3,6,7168]{3,2,1,0:T(8,128)(2,1)} %all_to_all.29) | data formatting | bytes 16515072 | tf_op jit(solution)/shard_map/reshape | solution.py:109
  381.5 6.7 fusion.35
  388.2 17.4 %convolution_convert_fusion = bf16[576,7168]{1,0:T(8,128)(2,1)} fusion(bf16[256,7168]{1,0:T(8,128)(2,1)} %param.21, bf16[576,7168]{1,0:T(8,128)(2,1)} %reshape.218, bf16[7168,256]{1,0:T(8,128)(2,1)} %param.20, f32[576,256]{1,0:T(8,128)S(1)} %fusion.35), kind=kOutput, calls=%fused_computation.1 | convolution fusion | flops 4232871936 | bytes 24444928 | tf_op jit(solution)/shard_map/dot_general | solution.py:22
  405.6 11.6 %reshape.219 = bf16[32,3,6,7168]{3,2,1,0:T(8,128)(2,1)} reshape(bf16[576,7168]{1,0:T(8,128)(2,1)} %convolution_convert_fusion) | data formatting | bytes 16515072 | tf_op jit(solution)/shard_map/reshape | solution.py:111
  417.2 132.9 %all_to_all.30 = bf16[32,3,6,7168]{3,2,1,0:T(8,128)(2,1)S(1)} all-to-all(bf16[32,3,6,7168]{3,2,1,0:T(8,128)(2,1)} %reshape.219), channel_id=1, replica_groups=mesh['sec'=4,'dev'=32] {'dev'}, dimensions={0} | all-to-all | bytes 16515072 | tf_op jit(solution)/shard_map/all_to_all | solution.py:110
  551.1 3.1 copy.57
  554.2 1.5 collective-permute-start.3
  555.7 3.1 copy.58
  558.7 1.4 collective-permute-start.4
  560.1 3.2 copy.59
  564.7 105.6 %collective-permute-done.4 = bf16[32,6,7168]{2,0,1:T(8,128)(2,1)} collective-permute-done((bf16[32,6,7168]{2,0,1:T(8,128)(2,1)}, bf16[32,6,7168]{2,0,1:T(8,128)(2,1)}, u32[]{:S(2)}, u32[]{:S(2)}) %collective-permute-start.4) | collective-permute-done | bytes 2752544 | tf_op jit(solution)/shard_map/ppermute | solution.py:15
  670.3 7.0 %collective-permute-done.5 = bf16[32,6,7168]{2,0,1:T(8,128)(2,1)} collective-permute-done((bf16[32,6,7168]{2,0,1:T(8,128)(2,1)}, bf16[32,6,7168]{2,0,1:T(8,128)(2,1)}, u32[]{:S(2)}, u32[]{:S(2)}) %collective-permute-start.5) | collective-permute-done | bytes 2752544 | tf_op jit(solution)/shard_map/ppermute | solution.py:15
  677.3 4.4 convert_reduce_fusion
  682.3 2.0 fusion.3
  (49 shorter events, 10.3 us)
Async XLA Ops:
  6.5 1.1 copy-start
  6.5 208.6 %reduce-scatter.2.cloned.1.call-start = ((), (), s32[]{:S(2)}) async-start(), calls=%async_computation.4 | async-start | bytes 3784704 | tf_op jit(solution)/shard_map/reduce_scatter | solution.py:66
  13.6 28.6 %copy-start.7 = (bf16[2,512,128]{2,1,0:T(8,128)(2,1)S(1)}, bf16[2,512,128]{2,1,0:T(8,128)(2,1)}, u32[]{:S(2)}) copy-start(bf16[2,512,128]{2,1,0:T(8,128)(2,1)} %param.17) | copy-start | bytes 786436
  20.3 22.2 %copy-start.2 = (bf16[256,7168]{1,0:T(8,128)(2,1)S(1)}, bf16[256,7168]{1,0:T(8,128)(2,1)}, u32[]{:S(2)}) copy-start(bf16[256,7168]{1,0:T(8,128)(2,1)} %param.18) | copy-start | bytes 11010052
  45.5 0.7 copy-start.5
  45.5 169.6 %copy-start.3 = (bf16[8,7168]{1,0:T(8,128)(2,1)S(1)}, bf16[8,7168]{1,0:T(8,128)(2,1)}, u32[]{:S(2)}) copy-start(bf16[8,7168]{1,0:T(8,128)(2,1)} %param.15) | copy-start | bytes 344068
  45.5 170.7 %copy-start.4 = (f32[7168]{0:T(1024)S(1)}, f32[7168]{0:T(1024)}, u32[]{:S(2)}) copy-start(f32[7168]{0:T(1024)} %param.16) | copy-start | bytes 86020
  217.4 6.3 collective-permute-start
  218.7 11.4 %collective-permute-start.1 = (bf16[24,7168]{1,0:T(8,128)(2,1)S(1)}, bf16[24,7168]{1,0:T(8,128)(2,1)S(1)}, u32[]{:S(2)}, u32[]{:S(2)}) collective-permute-start(bf16[24,7168]{1,0:T(8,128)(2,1)S(1)} %fusion.1), channel_id=1, source_target_pairs={{0,64},{32,96},{1,65},{33,97},{2,66},{34,98},{3,67},{35,99},{4,68}... | collective-permute-start | bytes 1032200 | tf_op jit(solution)/shard_map/ppermute | solution.py:15
  222.3 7.9 %collective-permute-start.2 = (bf16[24,7168]{1,0:T(8,128)(2,1)S(1)}, bf16[24,7168]{1,0:T(8,128)(2,1)S(1)}, u32[]{:S(2)}, u32[]{:S(2)}) collective-permute-start(bf16[24,7168]{1,0:T(8,128)(2,1)S(1)} %fusion.1), channel_id=1, source_target_pairs={{0,32},{32,64},{64,96},{1,33},{33,65},{65,97},{2,34},{34,66},{66,9... | collective-permute-start | bytes 1032200 | tf_op jit(solution)/shard_map/ppermute | solution.py:15
  554.2 10.6 %collective-permute-start.3 = (bf16[32,6,7168]{2,0,1:T(8,128)(2,1)}, bf16[32,6,7168]{2,0,1:T(8,128)(2,1)S(1)}, u32[]{:S(2)}, u32[]{:S(2)}) collective-permute-start(bf16[32,6,7168]{2,0,1:T(8,128)(2,1)} %copy.57), channel_id=1, source_target_pairs={{32,0},{64,32},{96,64},{33,1},{65,33},{97,65},{34,2},{66,34},{98,6... | collective-permute-start | bytes 8257544 | tf_op jit(solution)/shard_map/ppermute | solution.py:15
  558.7 5.9 copy-start.6
  558.7 111.6 %collective-permute-start.4 = (bf16[32,6,7168]{2,0,1:T(8,128)(2,1)}, bf16[32,6,7168]{2,0,1:T(8,128)(2,1)}, u32[]{:S(2)}, u32[]{:S(2)}) collective-permute-start(bf16[32,6,7168]{2,0,1:T(8,128)(2,1)} %copy.58), channel_id=1, source_target_pairs={{64,0},{96,32},{65,1},{97,33},{66,2},{98,34},{67,3},{99,35},{68,4}... | collective-permute-start | bytes 8257544 | tf_op jit(solution)/shard_map/ppermute | solution.py:15
  563.3 114.0 %collective-permute-start.5 = (bf16[32,6,7168]{2,0,1:T(8,128)(2,1)}, bf16[32,6,7168]{2,0,1:T(8,128)(2,1)}, u32[]{:S(2)}, u32[]{:S(2)}) collective-permute-start(bf16[32,6,7168]{2,0,1:T(8,128)(2,1)} %copy.59), channel_id=1, source_target_pairs={{96,0},{97,1},{98,2},{99,3},{100,4},{101,5},{102,6},{103,7},{104,8... | collective-permute-start | bytes 8257544 | tf_op jit(solution)/shard_map/ppermute | solution.py:15
  677.3 7.0 %copy-start.1 = (bf16[8,64,576]{2,1,0:T(8,128)(2,1)S(1)}, bf16[8,64,576]{2,1,0:T(8,128)(2,1)}, u32[]{:S(2)}) copy-start(bf16[8,64,576]{2,1,0:T(8,128)(2,1)} %param.12) | copy-start | bytes 1769476
Sparse Core Ops, SparseCore 0:
  45.6 169.4 reduce-scatter.1
where the time goes:
time: 692 us; the launch traced here: 691 us
  blocking collectives  287 us (41%)
  waiting for transfers between devices  287 us (41%)
  matrix products  43.2 us (6%)
  local copies, waits for them, and re-layouts  42.3 us (6%)
  between operations  13.6 us (2%)
  starting transfers between devices  10.4 us (2%)
  other arithmetic  7.04 us (1%)
    reduce_scatter x1, waiting for transfers between devices, layer_block(): lax.psum_scatter(jnp.dot(head_flat, out_weight, preferred_element_type=jn...  168 us
    all_to_all x1, blocking collectives, layer_block(): lax.all_to_all(partial_out.reshape(group_size, last_section, slot_width,...  133 us
    all_to_all x1, blocking collectives, layer_block(): lax.all_to_all(spread, 'dev', split_axis=0, concat_axis=0, tiled=True)  133 us
    ppermute x6, waiting for transfers between devices, from_behind(): return lax.ppermute(x, axis, pairs)  119 us
    all_to_all x1, blocking collectives, layer_block(): lax.all_to_all(latent_out, 'dev', split_axis=1, concat_axis=0, tiled=True)  21.5 us
    dot_general x1, matrix products, expert_block(): jnp.dot(activated, down_weight, preferred_element_type=jnp.float32)  17.4 us
  transfers between devices with their start and end apart: 7, of which 4 were waited for; matrix products, arithmetic and copies ran while one was open for 1% of the time, Pallas kernels for 0%

commit v1 on v0

--- a/solution.py
+++ b/solution.py
@@ -7,6 +7,12 @@
 TOPK = 2
 MICRO = 2
 CAP = 3
+
+
+def stacked_exchange(block, name, split, join):
+    shards = jnp.split(block, lax.axis_size(name), axis=split)
+    arrived = lax.all_to_all(jnp.stack(shards), name, 0, 0)
+    return jnp.concatenate(arrived, axis=join)
 
 
 def from_behind(x, axis, by):
@@ -58,7 +64,7 @@
     latent_out = jnp.einsum(
         "thp,tpc->thc", weights, latent_cache, preferred_element_type=jnp.float32
     )[:, :, :latent_width].astype(jnp.bfloat16)
-    by_heads = lax.all_to_all(latent_out, "dev", split_axis=1, concat_axis=0, tiled=True)
+    by_heads = stacked_exchange(latent_out, "dev", 1, 0)
     head_out = jnp.einsum(
         "thc,hcv->thv", by_heads, value_up, preferred_element_type=jnp.float32
     ).astype(jnp.bfloat16)

time: 692 us -> 692 us (level)
  no operation moved by 1% of the time
where the time goes in v1:
time: 692 us; the launch traced here: 691 us
  blocking collectives  287 us (41%)
  waiting for transfers between devices  287 us (41%)
  matrix products  43.3 us (6%)
  local copies, waits for them, and re-layouts  42.9 us (6%)
  between operations  13.7 us (2%)
  starting transfers between devices  10.6 us (2%)
  other arithmetic  7.04 us (1%)
    reduce_scatter x1, waiting for transfers between devices, layer_block(): lax.psum_scatter(jnp.dot(head_flat, out_weight, preferred_element_type=jn...  168 us
    all_to_all x1, blocking collectives, layer_block(): lax.all_to_all(partial_out.reshape(group_size, last_section, slot_width,...  133 us
    all_to_all x1, blocking collectives, layer_block(): lax.all_to_all(spread, 'dev', split_axis=0, concat_axis=0, tiled=True)  132 us
    ppermute x6, waiting for transfers between devices, from_behind(): return lax.ppermute(x, axis, pairs)  119 us
    all_to_all x1, blocking collectives, stacked_exchange(): arrived = lax.all_to_all(jnp.stack(shards), name, 0, 0)  21.4 us
    dot_general x1, matrix products, expert_block(): jnp.dot(activated, down_weight, preferred_element_type=jnp.float32)  17.4 us
  transfers between devices with their start and end apart: 7, of which 4 were waited for; matrix products, arithmetic and copies ran while one was open for 1% of the time, Pallas kernels for 0%

profile of v1, /device:TPU:0, one launch (start us, length us, event | category | flops | bytes accessed | tf_op | source)
XLA Modules:
  0.0 691.2 jit_solution(14177672631491637753)
XLA Ops:
  7.6 6.0 fusion.30
  13.7 6.7 convolution_convert_fusion.2
  21.4 21.4 %all_to_all.15 = bf16[32,8,2,512]{3,2,1,0:T(2,128)(2,1)S(1)} all-to-all(bf16[32,8,2,512]{3,2,1,0:T(2,128)(2,1)S(1)} %constant_dynamic-update-slice_fusion), channel_id=1, replica_groups=mesh['sec'=4,'dev'=32] {'dev'}, dimensions={0} | all-to-all | bytes 1048576 | tf_op jit(solution)/shard_map/all_to_all | solution.py:14
  43.1 2.9 convolution_convert_fusion.1
  47.4 168.3 %reduce-scatter.2.cloned.1.call-done = bf16[8,7168]{1,0:T(8,128)(2,1)} async-done(((bf16[256,7168]{1,0:T(8,128)(2,1)}), bf16[8,7168]{1,0:T(8,128)(2,1)}) %reduce-scatter.2.cloned.1.call-update) | async-done | bytes 114704 | tf_op jit(solution)/shard_map/reduce_scatter | solution.py:72
  218.0 1.3 collective-permute-start
  219.3 3.8 collective-permute-start.1
  224.5 6.3 collective-permute-done.1
  231.5 5.4 broadcast_in_dim.67
  236.9 132.3 %all_to_all.16 = bf16[32,3,6,7168]{3,2,1,0:T(8,128)(2,1)} all-to-all(bf16[32,3,6,7168]{3,2,1,0:T(8,128)(2,1)} %bitcast.169), channel_id=1, replica_groups=mesh['sec'=4,'dev'=32] {'dev'}, dimensions={0} | all-to-all | bytes 16515072 | tf_op jit(solution)/shard_map/all_to_all | solution.py:114
  369.3 12.5 %reshape.222 = bf16[576,7168]{1,0:T(8,128)(2,1)} reshape(bf16[32,3,6,7168]{3,2,1,0:T(8,128)(2,1)} %all_to_all.16) | data formatting | bytes 16515072 | tf_op jit(solution)/shard_map/reshape | solution.py:115
  381.7 6.7 fusion.33
  388.4 17.4 %convolution_convert_fusion = bf16[576,7168]{1,0:T(8,128)(2,1)} fusion(bf16[256,7168]{1,0:T(8,128)(2,1)} %param.21, bf16[576,7168]{1,0:T(8,128)(2,1)} %reshape.222, bf16[7168,256]{1,0:T(8,128)(2,1)} %param.20, f32[576,256]{1,0:T(8,128)S(1)} %fusion.33), kind=kOutput, calls=%fused_computation.1 | convolution fusion | flops 4232871936 | bytes 24444928 | tf_op jit(solution)/shard_map/dot_general | solution.py:28
  405.8 11.6 %reshape.223 = bf16[32,3,6,7168]{3,2,1,0:T(8,128)(2,1)} reshape(bf16[576,7168]{1,0:T(8,128)(2,1)} %convolution_convert_fusion) | data formatting | bytes 16515072 | tf_op jit(solution)/shard_map/reshape | solution.py:117
  417.4 132.8 %all_to_all.17 = bf16[32,3,6,7168]{3,2,1,0:T(8,128)(2,1)S(1)} all-to-all(bf16[32,3,6,7168]{3,2,1,0:T(8,128)(2,1)} %reshape.223), channel_id=1, replica_groups=mesh['sec'=4,'dev'=32] {'dev'}, dimensions={0} | all-to-all | bytes 16515072 | tf_op jit(solution)/shard_map/all_to_all | solution.py:116
  551.2 3.1 copy.54
  554.2 1.5 collective-permute-start.3
  555.8 3.1 copy.55
  558.8 1.4 collective-permute-start.4
  560.2 3.2 copy.56
  564.8 105.5 %collective-permute-done.4 = bf16[32,6,7168]{2,0,1:T(8,128)(2,1)} collective-permute-done((bf16[32,6,7168]{2,0,1:T(8,128)(2,1)}, bf16[32,6,7168]{2,0,1:T(8,128)(2,1)}, u32[]{:S(2)}, u32[]{:S(2)}) %collective-permute-start.4) | collective-permute-done | bytes 2752544 | tf_op jit(solution)/shard_map/ppermute | solution.py:21
  670.3 7.1 %collective-permute-done.5 = bf16[32,6,7168]{2,0,1:T(8,128)(2,1)} collective-permute-done((bf16[32,6,7168]{2,0,1:T(8,128)(2,1)}, bf16[32,6,7168]{2,0,1:T(8,128)(2,1)}, u32[]{:S(2)}, u32[]{:S(2)}) %collective-permute-start.5) | collective-permute-done | bytes 2752544 | tf_op jit(solution)/shard_map/ppermute | solution.py:21
  677.4 4.4 convert_reduce_fusion
  682.3 2.0 fusion.3
  (79 shorter events, 10.8 us)
Async XLA Ops:
  6.5 1.1 copy-start
  6.5 209.1 %reduce-scatter.2.cloned.1.call-start = ((), (), s32[]{:S(2)}) async-start(), calls=%async_computation.4 | async-start | bytes 3784704 | tf_op jit(solution)/shard_map/reduce_scatter | solution.py:72
  13.6 29.2 %copy-start.7 = (bf16[2,512,128]{2,1,0:T(8,128)(2,1)S(1)}, bf16[2,512,128]{2,1,0:T(8,128)(2,1)}, u32[]{:S(2)}) copy-start(bf16[2,512,128]{2,1,0:T(8,128)(2,1)} %param.17) | copy-start | bytes 786436
  13.6 29.5 %copy-start.2 = (bf16[256,7168]{1,0:T(8,128)(2,1)S(1)}, bf16[256,7168]{1,0:T(8,128)(2,1)}, u32[]{:S(2)}) copy-start(bf16[256,7168]{1,0:T(8,128)(2,1)} %param.18) | copy-start | bytes 11010052
  46.1 0.7 copy-start.5
  46.1 169.6 %copy-start.3 = (bf16[8,7168]{1,0:T(8,128)(2,1)S(1)}, bf16[8,7168]{1,0:T(8,128)(2,1)}, u32[]{:S(2)}) copy-start(bf16[8,7168]{1,0:T(8,128)(2,1)} %param.15) | copy-start | bytes 344068
  46.1 170.7 %copy-start.4 = (f32[7168]{0:T(1024)S(1)}, f32[7168]{0:T(1024)}, u32[]{:S(2)}) copy-start(f32[7168]{0:T(1024)} %param.16) | copy-start | bytes 86020
  218.0 6.4 collective-permute-start
  219.3 11.5 %collective-permute-start.1 = (bf16[24,7168]{1,0:T(8,128)(2,1)S(1)}, bf16[24,7168]{1,0:T(8,128)(2,1)S(1)}, u32[]{:S(2)}, u32[]{:S(2)}) collective-permute-start(bf16[24,7168]{1,0:T(8,128)(2,1)S(1)} %fusion.1), channel_id=1, source_target_pairs={{0,64},{32,96},{1,65},{33,97},{2,66},{34,98},{3,67},{35,99},{4,68}... | collective-permute-start | bytes 1032200 | tf_op jit(solution)/shard_map/ppermute | solution.py:21
  223.1 7.9 %collective-permute-start.2 = (bf16[24,7168]{1,0:T(8,128)(2,1)S(1)}, bf16[24,7168]{1,0:T(8,128)(2,1)S(1)}, u32[]{:S(2)}, u32[]{:S(2)}) collective-permute-start(bf16[24,7168]{1,0:T(8,128)(2,1)S(1)} %fusion.1), channel_id=1, source_target_pairs={{0,32},{32,64},{64,96},{1,33},{33,65},{65,97},{2,34},{34,66},{66,9... | collective-permute-start | bytes 1032200 | tf_op jit(solution)/shard_map/ppermute | solution.py:21
  554.2 10.6 %collective-permute-start.3 = (bf16[32,6,7168]{2,0,1:T(8,128)(2,1)}, bf16[32,6,7168]{2,0,1:T(8,128)(2,1)S(1)}, u32[]{:S(2)}, u32[]{:S(2)}) collective-permute-start(bf16[32,6,7168]{2,0,1:T(8,128)(2,1)} %copy.54), channel_id=1, source_target_pairs={{32,0},{64,32},{96,64},{33,1},{65,33},{97,65},{34,2},{66,34},{98,6... | collective-permute-start | bytes 8257544 | tf_op jit(solution)/shard_map/ppermute | solution.py:21
  558.8 5.9 copy-start.6
  558.8 111.5 %collective-permute-start.4 = (bf16[32,6,7168]{2,0,1:T(8,128)(2,1)}, bf16[32,6,7168]{2,0,1:T(8,128)(2,1)}, u32[]{:S(2)}, u32[]{:S(2)}) collective-permute-start(bf16[32,6,7168]{2,0,1:T(8,128)(2,1)} %copy.55), channel_id=1, source_target_pairs={{64,0},{96,32},{65,1},{97,33},{66,2},{98,34},{67,3},{99,35},{68,4}... | collective-permute-start | bytes 8257544 | tf_op jit(solution)/shard_map/ppermute | solution.py:21
  563.4 113.9 %collective-permute-start.5 = (bf16[32,6,7168]{2,0,1:T(8,128)(2,1)}, bf16[32,6,7168]{2,0,1:T(8,128)(2,1)}, u32[]{:S(2)}, u32[]{:S(2)}) collective-permute-start(bf16[32,6,7168]{2,0,1:T(8,128)(2,1)} %copy.56), channel_id=1, source_target_pairs={{96,0},{97,1},{98,2},{99,3},{100,4},{101,5},{102,6},{103,7},{104,8... | collective-permute-start | bytes 8257544 | tf_op jit(solution)/shard_map/ppermute | solution.py:21
  677.4 7.0 %copy-start.1 = (bf16[8,64,576]{2,1,0:T(8,128)(2,1)S(1)}, bf16[8,64,576]{2,1,0:T(8,128)(2,1)}, u32[]{:S(2)}) copy-start(bf16[8,64,576]{2,1,0:T(8,128)(2,1)} %param.12) | copy-start | bytes 1769476
Sparse Core Ops, SparseCore 0:
  46.2 169.3 reduce-scatter.1
